TPU v7x, 512 devices: a whole 4x4x16 slice. The times are simulated.
512 devices in a mesh: space: 32 (over z, core), tm: 16 (over x, y).
Axes of the slice: x: 4, y: 4, z: 16, core: 2. Of those that a mesh axis runs over, the one named last changes fastest.
Arguments:
- recordings: bfloat16 [2, 3, 512, 32768], P(None, None, 'space', 'tm'), may hold values from -30 to 30
- owner: int32 [512, 1], P('space'), may hold values from 0 to 31; in each aligned block of 16 rows (0 to 15, 16 to 31, ...) at most 2 rows name the same one
- valid_range: int32 [512, 2], P('space'), may hold values from 0 to 32768, as said below
- bin_mask: int32 [512, 96], P('space'), may hold values 0 or 1
Outputs:
- adjoint: bfloat16 [3, 2048, 32768], P(None, 'space', 'tm')
Inputs may be any that keep to these rules, and one draw needn't show every extreme that they name: `owner`: among the 16 receivers listed on one index of space, no subdomain owns more than 2; some subdomain owns exactly 2 of them. `valid_range`: column 0 is below column 1 in every row.
All inputs are finite; a program needn't handle non-finite values. No bound on the sum of `bin_mask` on one device may be relied on, other than what follows from the above.
Results may differ from a plain program's by a relative error of at most 0.013.
Values may be sent and summed in bfloat16 or wider, within the bound.
A program may use at most 128 MiB of HBM per device.

v0:
```python
import math
import jax
import jax.numpy as jnp
from jax import lax
from jax.sharding import PartitionSpec as P

BINS = 96
HOP = 256
HALO = 1024
KERNEL = 2304
WATER = 0.1
EPSILON = 1e-06


def with_halo(block, sides, width):
    for axis, dim in sides:
        count = lax.axis_size(axis)
        forward = [(i, i + 1) for i in range(count - 1)]
        backward = [(target, source) for source, target in forward]
        low = lax.ppermute(
            lax.slice_in_dim(block, block.shape[dim] - width, None, axis=dim), axis, forward
        )
        high = lax.ppermute(lax.slice_in_dim(block, 0, width, axis=dim), axis, backward)
        block = jnp.concatenate([low, block, high], axis=dim)
    return block


def shifted(block, axis, distance):
    devices = range(lax.axis_size(axis))
    route = [(i - distance, i) for i in devices if i - distance in devices]
    return lax.ppermute(block, axis, route)


def cq_kernel(kern_len, bins):
    octave_bins = bins // 8
    index = jnp.arange(bins).astype(jnp.float32)
    freq = 0.25 * jnp.exp2((index - (bins - 1)) / octave_bins)
    quality = 1.0 / (2.0 ** (1.0 / octave_bins) - 1.0)
    support = jnp.minimum(quality / freq, float(kern_len))
    offset = jnp.arange(kern_len).astype(jnp.float32) - 0.5 * (kern_len - 1)
    ratio = offset[:, None] / support[None, :]
    window = jnp.where(jnp.abs(ratio) < 0.5, 0.5 + 0.5 * jnp.cos(2.0 * math.pi * ratio), 0.0)
    window = window / jnp.sqrt(jnp.sum(window * window, axis=0, keepdims=True))
    cycles = offset[:, None] * freq[None, :]
    phase = cycles - jnp.floor(cycles)
    table = jnp.concatenate(
        [window * jnp.cos(2.0 * math.pi * phase), -window * jnp.sin(2.0 * math.pi * phase)], axis=1
    )
    return table.astype(jnp.bfloat16)


def adjoint_of(syn_re, syn_im, obs_re, obs_im, weight):
    level = (
        WATER * jnp.mean(obs_re * obs_re + obs_im * obs_im, axis=(-2, -1), keepdims=True) + EPSILON
    )
    syn_norm = jnp.sqrt(syn_re * syn_re + syn_im * syn_im + level)
    obs_norm = jnp.sqrt(obs_re * obs_re + obs_im * obs_im + level)
    diff_re = weight * (syn_re / syn_norm - obs_re / obs_norm)
    diff_im = weight * (syn_im / syn_norm - obs_im / obs_norm)
    inner = (syn_re * diff_re + syn_im * diff_im) / (syn_norm * syn_norm * syn_norm)
    return (diff_re / syn_norm - syn_re * inner, diff_im / syn_norm - syn_im * inner)


def analyse(blocks, table, frames):
    taps = table.shape[0] // HOP
    unfolded = jnp.concatenate([blocks[..., tap : tap + frames, :] for tap in range(taps)], axis=-1)
    return jnp.einsum("...fh,hk->...fk", unfolded, table, preferred_element_type=jnp.float32)


def synthesise(coefs, table, frames):
    taps = table.shape[0] // HOP
    term = jnp.einsum("...fk,hk->...fh", coefs, table, preferred_element_type=jnp.float32)
    term = term.reshape(term.shape[:-1] + (taps, HOP))
    lead = len(term.shape) - 3
    ext = jnp.zeros(coefs.shape[:-2] + (frames + taps - 1, HOP), jnp.float32)
    for tap in range(taps):
        widths = [(0, 0)] * lead + [(tap, taps - 1 - tap), (0, 0)]
        ext = ext + jnp.pad(term[..., tap, :], widths)
    return ext


def frame_weight(ranges, masks, frames_all):
    centers = jnp.arange(frames_all, dtype=jnp.int32) * HOP + HOP // 2
    inside = (ranges[:, 0:1] <= centers[None, :]) & (centers[None, :] < ranges[:, 1:2])
    return inside.astype(jnp.float32)[:, :, None] * masks.astype(jnp.float32)[:, None, :]


def misfit(coefs, weight):
    adj_re, adj_im = adjoint_of(
        coefs[0, ..., :BINS],
        coefs[0, ..., BINS:],
        coefs[1, ..., :BINS],
        coefs[1, ..., BINS:],
        weight,
    )
    joined = jnp.concatenate([adj_re, adj_im], axis=-1)
    return joined.reshape(joined.shape[:2] + (joined.shape[2] * joined.shape[3],)).astype(
        jnp.bfloat16
    )


def on_device(recordings, owner, valid_range, bin_mask):
    table = cq_kernel(KERNEL, BINS)
    margin = HALO // HOP
    width = 2 * BINS
    groups = lax.axis_size("tm")
    comps = recordings.shape[1]
    rec_dev = recordings.shape[2]
    samples_dev = recordings.shape[3]
    frames_dev = samples_dev // HOP
    rec_group = rec_dev // groups
    first_row = lax.axis_index("tm") * rec_group
    ranges = lax.dynamic_slice_in_dim(valid_range, first_row, rec_group, 0)
    masks = lax.dynamic_slice_in_dim(bin_mask, first_row, rec_group, 0)
    extended = with_halo(recordings, (("tm", 3),), HALO)
    blocks = extended.reshape(2, comps, rec_dev, frames_dev + 2 * margin, HOP)
    coefs = analyse(blocks, table, frames_dev)
    packed = coefs.astype(jnp.bfloat16).reshape(2, comps, rec_dev, frames_dev * width)
    weight = frame_weight(ranges, masks, frames_dev * groups)
    pieces = lax.all_to_all(packed, "tm", split_axis=2, concat_axis=3, tiled=True)
    items = pieces.shape[1]
    frames_all = pieces.shape[3] // width
    local_coefs = pieces.astype(jnp.float32).reshape(2, items, rec_group, frames_all, width)
    adjoint_local = misfit(local_coefs, weight)
    adjoint_back = lax.all_to_all(adjoint_local, "tm", split_axis=2, concat_axis=1, tiled=True)
    adjoint_frames = adjoint_back.reshape(comps, rec_dev, frames_dev, width)
    ext = synthesise(adjoint_frames, table, frames_dev)
    flat = ext.reshape(comps, rec_dev, (frames_dev + 2 * margin) * HOP)
    middle = flat[:, :, HALO : HALO + samples_dev]
    from_before = shifted(flat[:, :, HALO + samples_dev :].astype(jnp.bfloat16), "tm", 1).astype(
        jnp.float32
    )
    from_after = shifted(flat[:, :, :HALO].astype(jnp.bfloat16), "tm", -1).astype(jnp.float32)
    middle = middle.at[:, :, :HALO].add(from_before)
    middle = middle.at[:, :, samples_dev - HALO :].add(from_after)
    series = middle.astype(jnp.bfloat16)
    count = lax.axis_size("space")
    most = max(2, 3 * rec_dev // (2 * count))
    target = owner[:, 0]
    onehot = (target[:, None] == jnp.arange(count, dtype=jnp.int32)[None, :]).astype(jnp.int32)
    before = jnp.cumsum(onehot, axis=0) - onehot
    rank = jnp.sum(before * onehot, axis=1)
    slot = target * most + rank
    select = (jnp.arange(count * most, dtype=jnp.int32)[:, None] == slot[None, :]).astype(
        jnp.bfloat16
    )
    outgoing = jnp.einsum("sr,crt->cst", select, series, preferred_element_type=jnp.float32).astype(
        jnp.bfloat16
    )
    return lax.all_to_all(outgoing, "space", split_axis=1, concat_axis=1, tiled=True)


def solution(mesh):
    return jax.shard_map(
        on_device,
        mesh=mesh,
        in_specs=(
            P(None, None, "space", "tm"),
            P("space", None),
            P("space", None),
            P("space", None),
        ),
        out_specs=P(None, "space", "tm"),
        check_vma=False,
    )
```

profile of v0, /device:TPU:25, one launch (start us, length us, event | category | flops | bytes accessed | tf_op | source)
XLA Modules:
  0.0 347.0 jit_solution(11848009665123763137)
XLA Ops:
  0.0 1.1 fusion.24
  1.1 2.8 collective-permute-start
  3.9 2.5 collective-permute-start.1
  6.5 3.4 multiply_reduce_fusion
  9.9 6.7 %multiply_convert_fusion.3 = (bf16[2304,96]{0,1:T(8,128)(2,1)S(1)}, bf16[2304,96]{0,1:T(8,128)(2,1)S(1)}) fusion(f32[96]{0:T(128)S(1)} %get-tuple-element.51, f32[2304]{0:T(1024)S(1)} %convert_add_fusion.1, f32[96]{0:T(128)S(1)} %sqrt.38, f32[96]{0:T(128)S(1)} %get-tuple-element.50), kind=kLoop, calls=%fused_computation.19 | loop fusion | flops 3760128 | bytes 895104 | tf_op jit(solution)/shard_map/convert.7
  16.6 6.8 %multiply_convert_fusion.1 = (bf16[9,256,96]{1,2,0:T(8,128)(2,1)S(1)}, bf16[9,256,96]{1,2,0:T(8,128)(2,1)S(1)}) fusion(f32[96]{0:T(128)S(1)} %get-tuple-element.51, f32[9,256]{1,0:T(8,128)S(1)} %convert_add_fusion, f32[96]{0:T(128)S(1)} %sqrt.38, f32[96]{0:T(128)S(1)} %get-tuple-element.50), kind=kLoop, calls=%fused_computation.15 | loop fusion | flops 3760128 | bytes 895104 | tf_op jit(solution)/shard_map/convert.3
  23.5 0.7 fusion.19
  24.2 0.5 fusion.25
  24.8 0.2 copy.89
  25.0 0.1 slice_dynamic-update-slice_fusion.7
  25.1 0.1 slice_dynamic-update-slice_fusion.6
  25.3 0.1 slice_dynamic-update-slice_fusion.5
  25.4 0.1 slice_dynamic-update-slice_fusion.4
  25.5 0.1 slice_dynamic-update-slice_fusion.3
  25.6 0.1 slice_dynamic-update-slice_fusion.2
  25.8 0.1 slice_dynamic-update-slice_fusion.1
  25.9 1.1 convolution_convert_fusion.1
  27.0 0.3 reshape.520
  27.4 1.0 copy.61
  28.4 6.6 %all-to-all-start = ((bf16[2,3,16,1536]{3,0,1,2:T(2,128)(2,1)}), bf16[2,3,16,1536]{3,0,1,2:T(2,128)(2,1)S(1)}, u32[]{:S(2)}, u32[]{:S(2)}) async-start(bf16[2,3,16,1536]{3,0,1,2:T(2,128)(2,1)} %copy.61), calls=%async_computation | async-start | bytes 589824 | tf_op jit(solution)/shard_map/all_to_all | solution.py:120
  35.0 1.2 and_convert_fusion
  36.3 4.4 %all-to-all-done = bf16[2,3,16,1536]{3,0,1,2:T(2,128)(2,1)S(1)} async-done(((bf16[2,3,16,1536]{3,0,1,2:T(2,128)(2,1)}), bf16[2,3,16,1536]{3,0,1,2:T(2,128)(2,1)S(1)}, u32[]{:S(2)}, u32[]{:S(2)}) %all-to-all-start) | async-done | bytes 294944 | tf_op jit(solution)/shard_map/all_to_all | solution.py:120
  40.8 0.2 reshape.523
  41.0 0.2 fusion.22
  41.2 0.4 subtract_convert_fusion.1
  41.6 0.1 pad_maximum_fusion.1
  41.7 0.2 convert_element_type.135
  42.0 19.4 %copy.66 = bf16[3,1,24576]{0,1,2:T(2,128)(2,1)} copy(bf16[3,1,24576]{2,0,1:T(4,128)(2,1)S(1)} %convert_element_type.135) | data formatting | bytes 294912 | tf_op jit(solution)/shard_map/convert_element_type | solution.py:97
  61.4 0.5 broadcast.341
  61.9 134.9 %reduce.5 = bf16[24576,3]{1,0:T(8,128)(2,1)} reduce(bf16[24576,1,3]{2,1,0:T(2,128)(2,1)} %bitcast.152, bf16[]{:T(256)} %broadcast.341), dimensions={1}, to_apply=%bitcast.148.reduce_sub_computation | reduce | bytes 294914
  196.9 10.0 %reshape.529 = bf16[16,2,2304]{2,1,0:T(2,128)(2,1)} reshape(bf16[24576,3]{1,0:T(8,128)(2,1)} %reduce.5) | data formatting | bytes 294912
  206.9 5.5 %all-to-all-start.1 = ((bf16[16,2,2304]{2,1,0:T(2,128)(2,1)}), bf16[16,2,2304]{2,1,0:T(2,128)(2,1)S(1)}, u32[]{:S(2)}, u32[]{:S(2)}) async-start(bf16[16,2,2304]{2,1,0:T(2,128)(2,1)} %reshape.529), calls=%async_computation.1 | async-start | bytes 294912 | tf_op jit(solution)/shard_map/all_to_all | solution.py:125
  212.5 0.2 select_reduce_fusion
  212.7 4.8 %all-to-all-done.1 = bf16[16,2,2304]{2,1,0:T(2,128)(2,1)S(1)} async-done(((bf16[16,2,2304]{2,1,0:T(2,128)(2,1)}), bf16[16,2,2304]{2,1,0:T(2,128)(2,1)S(1)}, u32[]{:S(2)}, u32[]{:S(2)}) %all-to-all-start.1) | async-done | bytes 147488 | tf_op jit(solution)/shard_map/all_to_all | solution.py:125
  217.5 14.4 %reshape.530 = bf16[24576,1,3]{2,1,0:T(2,128)(2,1)} reshape(bf16[16,2,2304]{2,1,0:T(2,128)(2,1)S(1)} %all-to-all-done.1) | data formatting | bytes 294912
  231.9 23.3 %copy.67 = bf16[3,1,24576]{2,0,1:T(4,128)(2,1)S(1)} copy(bf16[3,1,24576]{0,1,2:T(2,128)(2,1)} %bitcast.151) | data formatting | bytes 294912 | tf_op jit(solution)/shard_map/all_to_all | solution.py:125
  255.2 0.2 reshape.525
  255.4 0.6 fusion.5
  256.1 0.4 slice_bitcast_fusion.8
  256.5 0.5 pad_add_fusion
  257.1 0.1 reshape.522
  257.3 3.5 %collective-permute-start.2 = (bf16[3,16,1024]{2,1,0:T(8,128)(2,1)S(1)}, bf16[3,16,1024]{2,1,0:T(8,128)(2,1)S(1)}, u32[]{:S(2)}, u32[]{:S(2)}) collective-permute-start(bf16[3,16,1024]{2,1,0:T(8,128)(2,1)S(1)} %get-tuple-element.41), channel_id=1, source_target_pairs={{0,1},{1,2},{2,3},{3,4},{4,5},{5,6},{6,7},{7,8},{8,9},{9,10},{10,1... | collective-permute-start | bytes 294920 | tf_op jit(solution)/shard_map/ppermute | solution.py:31
  260.9 1.9 collective-permute-start.3
  262.8 5.5 %collective-permute-done.3 = bf16[3,16,1024]{2,1,0:T(8,128)(2,1)S(1)} collective-permute-done((bf16[3,16,1024]{2,1,0:T(8,128)(2,1)S(1)}, bf16[3,16,1024]{2,1,0:T(8,128)(2,1)S(1)}, u32[]{:S(2)}, u32[]{:S(2)}) %collective-permute-start.3) | collective-permute-done | bytes 98336 | tf_op jit(solution)/shard_map/ppermute | solution.py:31
  268.4 0.5 fusion
  268.9 0.7 copy.76
  269.5 76.0 %all_to_all.23 = bf16[3,64,2048]{2,0,1:T(4,128)(2,1)S(1)} all-to-all(bf16[3,64,2048]{2,0,1:T(4,128)(2,1)S(1)} %copy.76), channel_id=1, replica_groups=mesh['space'=32,'tm'=16] {'space'}, dimensions={1} | all-to-all | bytes 1572864 | tf_op jit(solution)/shard_map/all_to_all | solution.py:150
  345.5 1.5 copy.77
  (28 shorter events, 0.6 us)
Async XLA Ops:
  0.0 23.4 %copy-start = (s32[16,2]{0,1:T(2,128)S(1)}, s32[16,2]{0,1:T(2,128)}, u32[]{:S(2)}) copy-start(s32[16,2]{0,1:T(2,128)} %param.10) | copy-start | bytes 388
  0.0 24.7 %copy-start.1 = (bf16[2,3,16,2048]{3,2,1,0:T(8,128)(2,1)S(1)}, bf16[2,3,16,2048]{3,2,1,0:T(8,128)(2,1)}, u32[]{:S(2)}) copy-start(bf16[2,3,16,2048]{3,2,1,0:T(8,128)(2,1)} %param.8) | copy-start | bytes 1179652
  1.1 23.6 %collective-permute-start = (bf16[2,3,16,1024]{3,2,1,0:T(8,128)(2,1)S(1)}, bf16[2,3,16,1024]{3,2,1,0:T(8,128)(2,1)S(1)}, u32[]{:S(2)}, u32[]{:S(2)}) collective-permute-start(bf16[2,3,16,1024]{3,2,1,0:T(8,128)(2,1)S(1)} %get-tuple-element.42), channel_id=1, source_target_pairs={{0,1},{1,2},{2,3},{3,4},{4,5},{5,6},{6,7},{7,8},{8,9},{9,10},{10,1... | collective-permute-start | bytes 589832 | tf_op jit(solution)/shard_map/ppermute | solution.py:20
  3.9 20.8 %collective-permute-start.1 = (bf16[2,3,16,1024]{3,2,1,0:T(8,128)(2,1)S(1)}, bf16[2,3,16,1024]{3,2,1,0:T(8,128)(2,1)S(1)}, u32[]{:S(2)}, u32[]{:S(2)}) collective-permute-start(bf16[2,3,16,1024]{3,2,1,0:T(8,128)(2,1)S(1)} %get-tuple-element.43), channel_id=1, source_target_pairs={{1,0},{2,1},{3,2},{4,3},{5,4},{6,5},{7,6},{8,7},{9,8},{10,9},{11,1... | collective-permute-start | bytes 589832 | tf_op jit(solution)/shard_map/ppermute | solution.py:23
  28.4 12.3 %all-to-all-start = ((bf16[2,3,16,1536]{3,0,1,2:T(2,128)(2,1)}), bf16[2,3,16,1536]{3,0,1,2:T(2,128)(2,1)S(1)}, u32[]{:S(2)}, u32[]{:S(2)}) async-start(bf16[2,3,16,1536]{3,0,1,2:T(2,128)(2,1)} %copy.61), calls=%async_computation | async-start | bytes 589824 | tf_op jit(solution)/shard_map/all_to_all | solution.py:120
  196.9 15.5 %copy-start.2 = (s32[16,1]{0,1:T(1,128)S(1)}, s32[16,1]{0,1:T(1,128)}, u32[]{:S(2)}) copy-start(s32[16,1]{0,1:T(1,128)} %param.9) | copy-start | bytes 196
  206.9 10.6 %all-to-all-start.1 = ((bf16[16,2,2304]{2,1,0:T(2,128)(2,1)}), bf16[16,2,2304]{2,1,0:T(2,128)(2,1)S(1)}, u32[]{:S(2)}, u32[]{:S(2)}) async-start(bf16[16,2,2304]{2,1,0:T(2,128)(2,1)} %reshape.529), calls=%async_computation.1 | async-start | bytes 294912 | tf_op jit(solution)/shard_map/all_to_all | solution.py:125
  257.3 5.5 %collective-permute-start.2 = (bf16[3,16,1024]{2,1,0:T(8,128)(2,1)S(1)}, bf16[3,16,1024]{2,1,0:T(8,128)(2,1)S(1)}, u32[]{:S(2)}, u32[]{:S(2)}) collective-permute-start(bf16[3,16,1024]{2,1,0:T(8,128)(2,1)S(1)} %get-tuple-element.41), channel_id=1, source_target_pairs={{0,1},{1,2},{2,3},{3,4},{4,5},{5,6},{6,7},{7,8},{8,9},{9,10},{10,1... | collective-permute-start | bytes 294920 | tf_op jit(solution)/shard_map/ppermute | solution.py:31
  260.9 7.5 %collective-permute-start.3 = (bf16[3,16,1024]{2,1,0:T(8,128)(2,1)S(1)}, bf16[3,16,1024]{2,1,0:T(8,128)(2,1)S(1)}, u32[]{:S(2)}, u32[]{:S(2)}) collective-permute-start(bf16[3,16,1024]{2,1,0:T(8,128)(2,1)S(1)} %get-tuple-element.40), channel_id=1, source_target_pairs={{1,0},{2,1},{3,2},{4,3},{5,4},{6,5},{7,6},{8,7},{9,8},{10,9},{11,1... | collective-permute-start | bytes 294920 | tf_op jit(solution)/shard_map/ppermute | solution.py:31
where the time goes:
time: 348 us; the launch traced here: 347 us
  other arithmetic  156 us (45%)
  blocking collectives  76 us (22%)
  local copies, waits for them, and re-layouts  75.2 us (22%)
  starting transfers between devices  22.8 us (7%)
  waiting for transfers between devices  14.8 us (4%)
    unnamed x1, other arithmetic  135 us
    all_to_all x1, blocking collectives, on_device(): lax.all_to_all(outgoing, 'space', split_axis=1, concat_axis=1, tiled=True)  76 us
    unnamed x18, local copies, waits for them, and re-layouts  26 us
    all_to_all x1, local copies, waits for them, and re-layouts, on_device(): lax.all_to_all(adjoint_local, 'tm', split_axis=2, concat_axis=1, tiled=True)  23.3 us
    convert_element_type x2, local copies, waits for them, and re-layouts, misfit(): joined.reshape(joined.shape[:2] + (joined.shape[2] * joined.shape[3],))  19.7 us
    another operation x4, other arithmetic  13.9 us
  transfers between devices with their start and end apart: 6, of which 3 were waited for; matrix products, arithmetic and copies ran while one was open for 6% of the time, Pallas kernels for 0%

commit v1 on v0

--- a/solution.py
+++ b/solution.py
@@ -10,6 +10,31 @@
 KERNEL = 2304
 WATER = 0.1
 EPSILON = 1e-06
+
+
+def produce_side(t0, dimension_no, x_local):
+    h_now = t0.shape
+    answer = t0.reshape(
+        *h_now[:dimension_no], x_local, h_now[dimension_no] // x_local, *h_now[dimension_no + 1 :]
+    )
+    return jnp.moveaxis(answer, dimension_no, 0)
+
+
+def _put_area(original, which_dim):
+    r1 = list(original.shape[1:])
+    r1[which_dim] *= original.shape[0]
+    return jnp.moveaxis(original, 0, which_dim).reshape(r1)
+
+
+def show_quarters(in_array, mesh_ax, v0, frame_in=1):
+    opened, arr_now = (lax.axis_size(mesh_ax), lax.axis_index(mesh_ax))
+    s_next = produce_side(in_array, v0, opened)
+    trail = [s_next[arr_now]]
+    for s in range(1, opened):
+        v1 = s_next[arr_now ^ s]
+        trail.append(lax.ppermute(v1, axis_name=mesh_ax, perm=[(m, m ^ s) for m in range(opened)]))
+    s_next = jnp.stack(trail)[arr_now ^ jnp.arange(opened)]
+    return _put_area(s_next, frame_in)
 
 
 def with_halo(block, sides, width):
@@ -122,7 +147,7 @@
     frames_all = pieces.shape[3] // width
     local_coefs = pieces.astype(jnp.float32).reshape(2, items, rec_group, frames_all, width)
     adjoint_local = misfit(local_coefs, weight)
-    adjoint_back = lax.all_to_all(adjoint_local, "tm", split_axis=2, concat_axis=1, tiled=True)
+    adjoint_back = show_quarters(adjoint_local, "tm", 2)
     adjoint_frames = adjoint_back.reshape(comps, rec_dev, frames_dev, width)
     ext = synthesise(adjoint_frames, table, frames_dev)
     flat = ext.reshape(comps, rec_dev, (frames_dev + 2 * margin) * HOP)

time: 348 us -> 199 us (0.57)
  other arithmetic: 156 us -> 20.8 us
  local copies, waits for them, and re-layouts: 75.2 us -> 8.96 us
  starting transfers between devices: 22.8 us -> 73.1 us
    unnamed x1 -> x0, other arithmetic: 135 us -> none
    ppermute x0 -> x15, starting transfers between devices: none -> 55.9 us  [show_quarters(): lax.ppermute(v1, axis_name=mesh_ax, perm=[(m, m ^ s) for m in range(opene...]
    unnamed x18 -> x45, local copies, waits for them, and re-layouts: 26 us -> 1.35 us
    all_to_all x1 -> x0, local copies, waits for them, and re-layouts: 23.3 us -> none  [on_device(): lax.all_to_all(adjoint_local, 'tm', split_axis=2, concat_axis=1, tiled=True)]
    convert_element_type x2 -> x1, local copies, waits for them, and re-layouts: 19.7 us -> 0.17 us  [misfit(): joined.reshape(joined.shape[:2] + (joined.shape[2] * joined.shape[3],))]
    all_to_all x1 -> x0, starting transfers between devices: 5.49 us -> none  [on_device(): lax.all_to_all(adjoint_local, 'tm', split_axis=2, concat_axis=1, tiled=True)]
    all_to_all x1 -> x0, waiting for transfers between devices: 4.83 us -> none  [on_device(): lax.all_to_all(adjoint_local, 'tm', split_axis=2, concat_axis=1, tiled=True)]
    ppermute x0 -> x15, waiting for transfers between devices: none -> 3.48 us  [show_quarters(): lax.ppermute(v1, axis_name=mesh_ax, perm=[(m, m ^ s) for m in range(opene...]
  transfers between devices with their start and end apart: 6 -> 20, of which waited for: 3 -> 3; matrix products, arithmetic and copies ran while one was open for 6% -> 10% of each run, Pallas kernels for 0% -> 0%
where the time goes in v1:
time: 199 us; the launch traced here: 197 us
  blocking collectives  79.4 us (40%)
  starting transfers between devices  73.1 us (37%)
  other arithmetic  20.8 us (10%)
  waiting for transfers between devices  11.8 us (6%)
  local copies, waits for them, and re-layouts  8.96 us (5%)
  matrix products  2.22 us (1%)
    all_to_all x1, blocking collectives, on_device(): lax.all_to_all(outgoing, 'space', split_axis=1, concat_axis=1, tiled=True)  79.4 us
    ppermute x15, starting transfers between devices, show_quarters(): lax.ppermute(v1, axis_name=mesh_ax, perm=[(m, m ^ s) for m in range(opene...  55.9 us
    another operation x4, other arithmetic  13.9 us
    all_to_all x1, starting transfers between devices, on_device(): lax.all_to_all(packed, 'tm', split_axis=2, concat_axis=3, tiled=True)  6.61 us
    ppermute x2, starting transfers between devices, shifted(): return lax.ppermute(block, axis, route)  5.28 us
    all_to_all x1, waiting for transfers between devices, on_device(): lax.all_to_all(packed, 'tm', split_axis=2, concat_axis=3, tiled=True)  4.26 us
    ppermute x2, waiting for transfers between devices, shifted(): return lax.ppermute(block, axis, route)  4.08 us
  transfers between devices with their start and end apart: 20, of which 3 were waited for; matrix products, arithmetic and copies ran while one was open for 10% of the time, Pallas kernels for 0%

profile of v1, /device:TPU:25, one launch (start us, length us, event | category | flops | bytes accessed | tf_op | source)
XLA Modules:
  0.0 197.1 jit_solution(11954985447455754521)
XLA Ops:
  0.0 1.1 fusion.25
  1.1 2.8 %collective-permute-start = (bf16[2,3,16,1024]{3,2,1,0:T(8,128)(2,1)S(1)}, bf16[2,3,16,1024]{3,2,1,0:T(8,128)(2,1)S(1)}, u32[]{:S(2)}, u32[]{:S(2)}) collective-permute-start(bf16[2,3,16,1024]{3,2,1,0:T(8,128)(2,1)S(1)} %get-tuple-element.42), channel_id=1, source_target_pairs={{0,1},{1,2},{2,3},{3,4},{4,5},{5,6},{6,7},{7,8},{8,9},{9,10},{10,1... | collective-permute-start | bytes 589832 | tf_op jit(solution)/shard_map/ppermute | solution.py:45
  3.9 2.5 %collective-permute-start.1 = (bf16[2,3,16,1024]{3,2,1,0:T(8,128)(2,1)S(1)}, bf16[2,3,16,1024]{3,2,1,0:T(8,128)(2,1)S(1)}, u32[]{:S(2)}, u32[]{:S(2)}) collective-permute-start(bf16[2,3,16,1024]{3,2,1,0:T(8,128)(2,1)S(1)} %get-tuple-element.43), channel_id=1, source_target_pairs={{1,0},{2,1},{3,2},{4,3},{5,4},{6,5},{7,6},{8,7},{9,8},{10,9},{11,1... | collective-permute-start | bytes 589832 | tf_op jit(solution)/shard_map/ppermute | solution.py:48
  6.5 3.4 %multiply_reduce_fusion = f32[96]{0:T(128)S(1)} fusion(f32[96]{0:T(128)S(1)} %get-tuple-element.66, f32[2304]{0:T(1024)S(1)} %convert_add_fusion.1), kind=kLoop, calls=%fused_computation.21 | loop fusion | flops 1990560 | bytes 9984 | tf_op jit(solution)/shard_map/reduce_sum | solution.py:68
  10.0 0.6 fusion.26
  10.6 6.6 %multiply_convert_fusion.3 = (bf16[2304,96]{0,1:T(8,128)(2,1)S(1)}, bf16[2304,96]{0,1:T(8,128)(2,1)S(1)}) fusion(f32[96]{0:T(128)S(1)} %get-tuple-element.67, f32[2304]{0:T(1024)S(1)} %convert_add_fusion.1, f32[96]{0:T(128)S(1)} %sqrt.38, f32[96]{0:T(128)S(1)} %get-tuple-element.66), kind=kLoop, calls=%fused_computation.20 | loop fusion | flops 3760128 | bytes 895104 | tf_op jit(solution)/shard_map/convert.7
  17.2 6.8 %multiply_convert_fusion.1 = (bf16[9,256,96]{1,2,0:T(8,128)(2,1)S(1)}, bf16[9,256,96]{1,2,0:T(8,128)(2,1)S(1)}) fusion(f32[96]{0:T(128)S(1)} %get-tuple-element.67, f32[9,256]{1,0:T(8,128)S(1)} %convert_add_fusion, f32[96]{0:T(128)S(1)} %sqrt.38, f32[96]{0:T(128)S(1)} %get-tuple-element.66), kind=kLoop, calls=%fused_computation.16 | loop fusion | flops 3760128 | bytes 895104 | tf_op jit(solution)/shard_map/convert.3
  24.2 0.7 fusion.20
  24.9 0.2 select_reduce_fusion
  26.3 1.1 convolution_convert_fusion.1
  27.4 0.3 reshape.562
  27.7 1.0 copy.76
  28.8 6.6 %all-to-all-start = ((bf16[2,3,16,1536]{3,0,1,2:T(2,128)(2,1)}), bf16[2,3,16,1536]{3,0,1,2:T(2,128)(2,1)S(1)}, u32[]{:S(2)}, u32[]{:S(2)}) async-start(bf16[2,3,16,1536]{3,0,1,2:T(2,128)(2,1)} %copy.76), calls=%async_computation | async-start | bytes 589824 | tf_op jit(solution)/shard_map/all_to_all | solution.py:145
  35.4 1.3 and_convert_fusion
  36.8 4.3 %all-to-all-done = bf16[2,3,16,1536]{3,0,1,2:T(2,128)(2,1)S(1)} async-done(((bf16[2,3,16,1536]{3,0,1,2:T(2,128)(2,1)}), bf16[2,3,16,1536]{3,0,1,2:T(2,128)(2,1)S(1)}, u32[]{:S(2)}, u32[]{:S(2)}) %all-to-all-start) | async-done | bytes 294944 | tf_op jit(solution)/shard_map/all_to_all | solution.py:145
  41.1 0.2 reshape.564
  41.4 0.2 fusion.23
  41.6 0.4 subtract_convert_fusion.1
  42.1 0.2 convert_element_type.136
  42.3 0.4 constant_dynamic-slice_fusion
  42.7 2.9 %collective-permute-start.2 = (bf16[3,1,1536]{2,0,1:T(4,128)(2,1)S(1)}, bf16[3,1,1536]{2,0,1:T(4,128)(2,1)S(1)}, u32[]{:S(2)}, u32[]{:S(2)}) collective-permute-start(bf16[3,1,1536]{2,0,1:T(4,128)(2,1)S(1)} %bitcast.264), channel_id=1, source_target_pairs={{0,1},{1,0},{2,3},{3,2},{4,5},{5,4},{6,7},{7,6},{8,9},{9,8},{10,11... | collective-permute-start | bytes 27656 | tf_op jit(solution)/shard_map/ppermute | solution.py:35
  45.7 4.0 %collective-permute-start.3 = (bf16[3,1,1536]{2,0,1:T(4,128)(2,1)S(1)}, bf16[3,1,1536]{2,0,1:T(4,128)(2,1)S(1)}, u32[]{:S(2)}, u32[]{:S(2)}) collective-permute-start(bf16[3,1,1536]{2,0,1:T(4,128)(2,1)S(1)} %bitcast.263), channel_id=1, source_target_pairs={{0,2},{1,3},{2,0},{3,1},{4,6},{5,7},{6,4},{7,5},{8,10},{9,11},{10,... | collective-permute-start | bytes 27656 | tf_op jit(solution)/shard_map/ppermute | solution.py:35
  49.7 2.6 %collective-permute-start.4 = (bf16[3,1,1536]{2,0,1:T(4,128)(2,1)S(1)}, bf16[3,1,1536]{2,0,1:T(4,128)(2,1)S(1)}, u32[]{:S(2)}, u32[]{:S(2)}) collective-permute-start(bf16[3,1,1536]{2,0,1:T(4,128)(2,1)S(1)} %bitcast.262), channel_id=1, source_target_pairs={{0,3},{1,2},{2,1},{3,0},{4,7},{5,6},{6,5},{7,4},{8,11},{9,10},{10,... | collective-permute-start | bytes 27656 | tf_op jit(solution)/shard_map/ppermute | solution.py:35
  52.4 2.1 %collective-permute-start.5 = (bf16[3,1,1536]{2,0,1:T(4,128)(2,1)S(1)}, bf16[3,1,1536]{2,0,1:T(4,128)(2,1)S(1)}, u32[]{:S(2)}, u32[]{:S(2)}) collective-permute-start(bf16[3,1,1536]{2,0,1:T(4,128)(2,1)S(1)} %bitcast.261), channel_id=1, source_target_pairs={{0,4},{1,5},{2,6},{3,7},{4,0},{5,1},{6,2},{7,3},{8,12},{9,13},{10,... | collective-permute-start | bytes 27656 | tf_op jit(solution)/shard_map/ppermute | solution.py:35
  54.5 2.7 %collective-permute-start.6 = (bf16[3,1,1536]{2,0,1:T(4,128)(2,1)S(1)}, bf16[3,1,1536]{2,0,1:T(4,128)(2,1)S(1)}, u32[]{:S(2)}, u32[]{:S(2)}) collective-permute-start(bf16[3,1,1536]{2,0,1:T(4,128)(2,1)S(1)} %bitcast.260), channel_id=1, source_target_pairs={{0,5},{1,4},{2,7},{3,6},{4,1},{5,0},{6,3},{7,2},{8,13},{9,12},{10,... | collective-permute-start | bytes 27656 | tf_op jit(solution)/shard_map/ppermute | solution.py:35
  57.4 5.0 %collective-permute-start.7 = (bf16[3,1,1536]{2,0,1:T(4,128)(2,1)S(1)}, bf16[3,1,1536]{2,0,1:T(4,128)(2,1)S(1)}, u32[]{:S(2)}, u32[]{:S(2)}) collective-permute-start(bf16[3,1,1536]{2,0,1:T(4,128)(2,1)S(1)} %bitcast.259), channel_id=1, source_target_pairs={{0,6},{1,7},{2,4},{3,5},{4,2},{5,3},{6,0},{7,1},{8,14},{9,15},{10,... | collective-permute-start | bytes 27656 | tf_op jit(solution)/shard_map/ppermute | solution.py:35
  62.4 3.8 %collective-permute-start.8 = (bf16[3,1,1536]{2,0,1:T(4,128)(2,1)S(1)}, bf16[3,1,1536]{2,0,1:T(4,128)(2,1)S(1)}, u32[]{:S(2)}, u32[]{:S(2)}) collective-permute-start(bf16[3,1,1536]{2,0,1:T(4,128)(2,1)S(1)} %bitcast.258), channel_id=1, source_target_pairs={{0,7},{1,6},{2,5},{3,4},{4,3},{5,2},{6,1},{7,0},{8,15},{9,14},{10,... | collective-permute-start | bytes 27656 | tf_op jit(solution)/shard_map/ppermute | solution.py:35
  66.2 3.1 %collective-permute-start.9 = (bf16[3,1,1536]{2,0,1:T(4,128)(2,1)S(1)}, bf16[3,1,1536]{2,0,1:T(4,128)(2,1)S(1)}, u32[]{:S(2)}, u32[]{:S(2)}) collective-permute-start(bf16[3,1,1536]{2,0,1:T(4,128)(2,1)S(1)} %bitcast.257), channel_id=1, source_target_pairs={{0,8},{1,9},{2,10},{3,11},{4,12},{5,13},{6,14},{7,15},{8,0},{9,1},... | collective-permute-start | bytes 27656 | tf_op jit(solution)/shard_map/ppermute | solution.py:35
  69.4 2.0 %collective-permute-start.10 = (bf16[3,1,1536]{2,0,1:T(4,128)(2,1)S(1)}, bf16[3,1,1536]{2,0,1:T(4,128)(2,1)S(1)}, u32[]{:S(2)}, u32[]{:S(2)}) collective-permute-start(bf16[3,1,1536]{2,0,1:T(4,128)(2,1)S(1)} %bitcast.256), channel_id=1, source_target_pairs={{0,9},{1,8},{2,11},{3,10},{4,13},{5,12},{6,15},{7,14},{8,1},{9,0},... | collective-permute-start | bytes 27656 | tf_op jit(solution)/shard_map/ppermute | solution.py:35
  71.4 7.3 %collective-permute-start.11 = (bf16[3,1,1536]{2,0,1:T(4,128)(2,1)S(1)}, bf16[3,1,1536]{2,0,1:T(4,128)(2,1)S(1)}, u32[]{:S(2)}, u32[]{:S(2)}) collective-permute-start(bf16[3,1,1536]{2,0,1:T(4,128)(2,1)S(1)} %bitcast.255), channel_id=1, source_target_pairs={{0,10},{1,11},{2,8},{3,9},{4,14},{5,15},{6,12},{7,13},{8,2},{9,3},... | collective-permute-start | bytes 27656 | tf_op jit(solution)/shard_map/ppermute | solution.py:35
  78.8 4.2 %collective-permute-start.12 = (bf16[3,1,1536]{2,0,1:T(4,128)(2,1)S(1)}, bf16[3,1,1536]{2,0,1:T(4,128)(2,1)S(1)}, u32[]{:S(2)}, u32[]{:S(2)}) collective-permute-start(bf16[3,1,1536]{2,0,1:T(4,128)(2,1)S(1)} %bitcast.254), channel_id=1, source_target_pairs={{0,11},{1,10},{2,9},{3,8},{4,15},{5,14},{6,13},{7,12},{8,3},{9,2},... | collective-permute-start | bytes 27656 | tf_op jit(solution)/shard_map/ppermute | solution.py:35
  83.0 2.5 %collective-permute-start.13 = (bf16[3,1,1536]{2,0,1:T(4,128)(2,1)S(1)}, bf16[3,1,1536]{2,0,1:T(4,128)(2,1)S(1)}, u32[]{:S(2)}, u32[]{:S(2)}) collective-permute-start(bf16[3,1,1536]{2,0,1:T(4,128)(2,1)S(1)} %bitcast.253), channel_id=1, source_target_pairs={{0,12},{1,13},{2,14},{3,15},{4,8},{5,9},{6,10},{7,11},{8,4},{9,5},... | collective-permute-start | bytes 27656 | tf_op jit(solution)/shard_map/ppermute | solution.py:35
  85.5 1.9 collective-permute-start.14
  87.5 7.6 %collective-permute-start.15 = (bf16[3,1,1536]{2,0,1:T(4,128)(2,1)S(1)}, bf16[3,1,1536]{2,0,1:T(4,128)(2,1)S(1)}, u32[]{:S(2)}, u32[]{:S(2)}) collective-permute-start(bf16[3,1,1536]{2,0,1:T(4,128)(2,1)S(1)} %bitcast.251), channel_id=1, source_target_pairs={{0,14},{1,15},{2,12},{3,13},{4,10},{5,11},{6,8},{7,9},{8,6},{9,7},... | collective-permute-start | bytes 27656 | tf_op jit(solution)/shard_map/ppermute | solution.py:35
  95.1 4.2 %collective-permute-start.16 = (bf16[3,1,1536]{2,0,1:T(4,128)(2,1)S(1)}, bf16[3,1,1536]{2,0,1:T(4,128)(2,1)S(1)}, u32[]{:S(2)}, u32[]{:S(2)}) collective-permute-start(bf16[3,1,1536]{2,0,1:T(4,128)(2,1)S(1)} %bitcast.250), channel_id=1, source_target_pairs={{0,15},{1,14},{2,13},{3,12},{4,11},{5,10},{6,9},{7,8},{8,7},{9,6},... | collective-permute-start | bytes 27656 | tf_op jit(solution)/shard_map/ppermute | solution.py:35
  99.4 3.4 %collective-permute-done.16 = bf16[3,1,1536]{2,0,1:T(4,128)(2,1)S(1)} collective-permute-done((bf16[3,1,1536]{2,0,1:T(4,128)(2,1)S(1)}, bf16[3,1,1536]{2,0,1:T(4,128)(2,1)S(1)}, u32[]{:S(2)}, u32[]{:S(2)}) %collective-permute-start.16) | collective-permute-done | bytes 9248 | tf_op jit(solution)/shard_map/ppermute | solution.py:35
  102.9 0.7 gather_fusion
  103.6 0.2 reshape.576
  103.8 0.6 fusion.5
  104.4 0.4 slice_bitcast_fusion.8
  104.9 0.5 pad_add_fusion
  105.7 1.9 collective-permute-start.17
  107.6 3.4 %collective-permute-start.18 = (bf16[3,16,1024]{2,1,0:T(8,128)(2,1)S(1)}, bf16[3,16,1024]{2,1,0:T(8,128)(2,1)S(1)}, u32[]{:S(2)}, u32[]{:S(2)}) collective-permute-start(bf16[3,16,1024]{2,1,0:T(8,128)(2,1)S(1)} %get-tuple-element.40), channel_id=1, source_target_pairs={{1,0},{2,1},{3,2},{4,3},{5,4},{6,5},{7,6},{8,7},{9,8},{10,9},{11,1... | collective-permute-start | bytes 294920 | tf_op jit(solution)/shard_map/ppermute | solution.py:56
  111.0 4.1 %collective-permute-done.18 = bf16[3,16,1024]{2,1,0:T(8,128)(2,1)S(1)} collective-permute-done((bf16[3,16,1024]{2,1,0:T(8,128)(2,1)S(1)}, bf16[3,16,1024]{2,1,0:T(8,128)(2,1)S(1)}, u32[]{:S(2)}, u32[]{:S(2)}) %collective-permute-start.18) | collective-permute-done | bytes 98336 | tf_op jit(solution)/shard_map/ppermute | solution.py:56
  115.2 0.5 fusion
  115.6 0.7 copy.91
  116.3 79.4 %all_to_all.14 = bf16[3,64,2048]{2,0,1:T(4,128)(2,1)S(1)} all-to-all(bf16[3,64,2048]{2,0,1:T(4,128)(2,1)S(1)} %copy.91), channel_id=1, replica_groups=mesh['space'=32,'tm'=16] {'space'}, dimensions={1} | all-to-all | bytes 1572864 | tf_op jit(solution)/shard_map/all_to_all | solution.py:175
  195.7 1.5 copy.92
  (86 shorter events, 2.3 us)
Async XLA Ops:
  0.0 9.9 %copy-start = (s32[16,2]{0,1:T(2,128)S(1)}, s32[16,2]{0,1:T(2,128)}, u32[]{:S(2)}) copy-start(s32[16,2]{0,1:T(2,128)} %param.10) | copy-start | bytes 388
  0.0 25.1 %copy-start.1 = (bf16[2,3,16,2048]{3,2,1,0:T(8,128)(2,1)S(1)}, bf16[2,3,16,2048]{3,2,1,0:T(8,128)(2,1)}, u32[]{:S(2)}) copy-start(bf16[2,3,16,2048]{3,2,1,0:T(8,128)(2,1)} %param.8) | copy-start | bytes 1179652
  0.0 24.1 %copy-start.2 = (s32[16,1]{0,1:T(1,128)S(1)}, s32[16,1]{0,1:T(1,128)}, u32[]{:S(2)}) copy-start(s32[16,1]{0,1:T(1,128)} %param.9) | copy-start | bytes 196
  1.1 24.0 %collective-permute-start = (bf16[2,3,16,1024]{3,2,1,0:T(8,128)(2,1)S(1)}, bf16[2,3,16,1024]{3,2,1,0:T(8,128)(2,1)S(1)}, u32[]{:S(2)}, u32[]{:S(2)}) collective-permute-start(bf16[2,3,16,1024]{3,2,1,0:T(8,128)(2,1)S(1)} %get-tuple-element.42), channel_id=1, source_target_pairs={{0,1},{1,2},{2,3},{3,4},{4,5},{5,6},{6,7},{7,8},{8,9},{9,10},{10,1... | collective-permute-start | bytes 589832 | tf_op jit(solution)/shard_map/ppermute | solution.py:45
  3.9 21.2 %collective-permute-start.1 = (bf16[2,3,16,1024]{3,2,1,0:T(8,128)(2,1)S(1)}, bf16[2,3,16,1024]{3,2,1,0:T(8,128)(2,1)S(1)}, u32[]{:S(2)}, u32[]{:S(2)}) collective-permute-start(bf16[2,3,16,1024]{3,2,1,0:T(8,128)(2,1)S(1)} %get-tuple-element.43), channel_id=1, source_target_pairs={{1,0},{2,1},{3,2},{4,3},{5,4},{6,5},{7,6},{8,7},{9,8},{10,9},{11,1... | collective-permute-start | bytes 589832 | tf_op jit(solution)/shard_map/ppermute | solution.py:48
  28.8 12.3 %all-to-all-start = ((bf16[2,3,16,1536]{3,0,1,2:T(2,128)(2,1)}), bf16[2,3,16,1536]{3,0,1,2:T(2,128)(2,1)S(1)}, u32[]{:S(2)}, u32[]{:S(2)}) async-start(bf16[2,3,16,1536]{3,0,1,2:T(2,128)(2,1)} %copy.76), calls=%async_computation | async-start | bytes 589824 | tf_op jit(solution)/shard_map/all_to_all | solution.py:145
  42.7 14.7 %collective-permute-start.2 = (bf16[3,1,1536]{2,0,1:T(4,128)(2,1)S(1)}, bf16[3,1,1536]{2,0,1:T(4,128)(2,1)S(1)}, u32[]{:S(2)}, u32[]{:S(2)}) collective-permute-start(bf16[3,1,1536]{2,0,1:T(4,128)(2,1)S(1)} %bitcast.264), channel_id=1, source_target_pairs={{0,1},{1,0},{2,3},{3,2},{4,5},{5,4},{6,7},{7,6},{8,9},{9,8},{10,11... | collective-permute-start | bytes 27656 | tf_op jit(solution)/shard_map/ppermute | solution.py:35
  45.7 16.7 %collective-permute-start.3 = (bf16[3,1,1536]{2,0,1:T(4,128)(2,1)S(1)}, bf16[3,1,1536]{2,0,1:T(4,128)(2,1)S(1)}, u32[]{:S(2)}, u32[]{:S(2)}) collective-permute-start(bf16[3,1,1536]{2,0,1:T(4,128)(2,1)S(1)} %bitcast.263), channel_id=1, source_target_pairs={{0,2},{1,3},{2,0},{3,1},{4,6},{5,7},{6,4},{7,5},{8,10},{9,11},{10,... | collective-permute-start | bytes 27656 | tf_op jit(solution)/shard_map/ppermute | solution.py:35
  49.7 16.5 %collective-permute-start.4 = (bf16[3,1,1536]{2,0,1:T(4,128)(2,1)S(1)}, bf16[3,1,1536]{2,0,1:T(4,128)(2,1)S(1)}, u32[]{:S(2)}, u32[]{:S(2)}) collective-permute-start(bf16[3,1,1536]{2,0,1:T(4,128)(2,1)S(1)} %bitcast.262), channel_id=1, source_target_pairs={{0,3},{1,2},{2,1},{3,0},{4,7},{5,6},{6,5},{7,4},{8,11},{9,10},{10,... | collective-permute-start | bytes 27656 | tf_op jit(solution)/shard_map/ppermute | solution.py:35
  52.4 17.0 %collective-permute-start.5 = (bf16[3,1,1536]{2,0,1:T(4,128)(2,1)S(1)}, bf16[3,1,1536]{2,0,1:T(4,128)(2,1)S(1)}, u32[]{:S(2)}, u32[]{:S(2)}) collective-permute-start(bf16[3,1,1536]{2,0,1:T(4,128)(2,1)S(1)} %bitcast.261), channel_id=1, source_target_pairs={{0,4},{1,5},{2,6},{3,7},{4,0},{5,1},{6,2},{7,3},{8,12},{9,13},{10,... | collective-permute-start | bytes 27656 | tf_op jit(solution)/shard_map/ppermute | solution.py:35
  54.5 16.9 %collective-permute-start.6 = (bf16[3,1,1536]{2,0,1:T(4,128)(2,1)S(1)}, bf16[3,1,1536]{2,0,1:T(4,128)(2,1)S(1)}, u32[]{:S(2)}, u32[]{:S(2)}) collective-permute-start(bf16[3,1,1536]{2,0,1:T(4,128)(2,1)S(1)} %bitcast.260), channel_id=1, source_target_pairs={{0,5},{1,4},{2,7},{3,6},{4,1},{5,0},{6,3},{7,2},{8,13},{9,12},{10,... | collective-permute-start | bytes 27656 | tf_op jit(solution)/shard_map/ppermute | solution.py:35
  57.4 21.4 %collective-permute-start.7 = (bf16[3,1,1536]{2,0,1:T(4,128)(2,1)S(1)}, bf16[3,1,1536]{2,0,1:T(4,128)(2,1)S(1)}, u32[]{:S(2)}, u32[]{:S(2)}) collective-permute-start(bf16[3,1,1536]{2,0,1:T(4,128)(2,1)S(1)} %bitcast.259), channel_id=1, source_target_pairs={{0,6},{1,7},{2,4},{3,5},{4,2},{5,3},{6,0},{7,1},{8,14},{9,15},{10,... | collective-permute-start | bytes 27656 | tf_op jit(solution)/shard_map/ppermute | solution.py:35
  62.4 20.6 %collective-permute-start.8 = (bf16[3,1,1536]{2,0,1:T(4,128)(2,1)S(1)}, bf16[3,1,1536]{2,0,1:T(4,128)(2,1)S(1)}, u32[]{:S(2)}, u32[]{:S(2)}) collective-permute-start(bf16[3,1,1536]{2,0,1:T(4,128)(2,1)S(1)} %bitcast.258), channel_id=1, source_target_pairs={{0,7},{1,6},{2,5},{3,4},{4,3},{5,2},{6,1},{7,0},{8,15},{9,14},{10,... | collective-permute-start | bytes 27656 | tf_op jit(solution)/shard_map/ppermute | solution.py:35
  66.2 19.3 %collective-permute-start.9 = (bf16[3,1,1536]{2,0,1:T(4,128)(2,1)S(1)}, bf16[3,1,1536]{2,0,1:T(4,128)(2,1)S(1)}, u32[]{:S(2)}, u32[]{:S(2)}) collective-permute-start(bf16[3,1,1536]{2,0,1:T(4,128)(2,1)S(1)} %bitcast.257), channel_id=1, source_target_pairs={{0,8},{1,9},{2,10},{3,11},{4,12},{5,13},{6,14},{7,15},{8,0},{9,1},... | collective-permute-start | bytes 27656 | tf_op jit(solution)/shard_map/ppermute | solution.py:35
  69.4 18.1 %collective-permute-start.10 = (bf16[3,1,1536]{2,0,1:T(4,128)(2,1)S(1)}, bf16[3,1,1536]{2,0,1:T(4,128)(2,1)S(1)}, u32[]{:S(2)}, u32[]{:S(2)}) collective-permute-start(bf16[3,1,1536]{2,0,1:T(4,128)(2,1)S(1)} %bitcast.256), channel_id=1, source_target_pairs={{0,9},{1,8},{2,11},{3,10},{4,13},{5,12},{6,15},{7,14},{8,1},{9,0},... | collective-permute-start | bytes 27656 | tf_op jit(solution)/shard_map/ppermute | solution.py:35
  71.4 23.7 %collective-permute-start.11 = (bf16[3,1,1536]{2,0,1:T(4,128)(2,1)S(1)}, bf16[3,1,1536]{2,0,1:T(4,128)(2,1)S(1)}, u32[]{:S(2)}, u32[]{:S(2)}) collective-permute-start(bf16[3,1,1536]{2,0,1:T(4,128)(2,1)S(1)} %bitcast.255), channel_id=1, source_target_pairs={{0,10},{1,11},{2,8},{3,9},{4,14},{5,15},{6,12},{7,13},{8,2},{9,3},... | collective-permute-start | bytes 27656 | tf_op jit(solution)/shard_map/ppermute | solution.py:35
  78.8 20.5 %collective-permute-start.12 = (bf16[3,1,1536]{2,0,1:T(4,128)(2,1)S(1)}, bf16[3,1,1536]{2,0,1:T(4,128)(2,1)S(1)}, u32[]{:S(2)}, u32[]{:S(2)}) collective-permute-start(bf16[3,1,1536]{2,0,1:T(4,128)(2,1)S(1)} %bitcast.254), channel_id=1, source_target_pairs={{0,11},{1,10},{2,9},{3,8},{4,15},{5,14},{6,13},{7,12},{8,3},{9,2},... | collective-permute-start | bytes 27656 | tf_op jit(solution)/shard_map/ppermute | solution.py:35
  83.0 16.3 %collective-permute-start.13 = (bf16[3,1,1536]{2,0,1:T(4,128)(2,1)S(1)}, bf16[3,1,1536]{2,0,1:T(4,128)(2,1)S(1)}, u32[]{:S(2)}, u32[]{:S(2)}) collective-permute-start(bf16[3,1,1536]{2,0,1:T(4,128)(2,1)S(1)} %bitcast.253), channel_id=1, source_target_pairs={{0,12},{1,13},{2,14},{3,15},{4,8},{5,9},{6,10},{7,11},{8,4},{9,5},... | collective-permute-start | bytes 27656 | tf_op jit(solution)/shard_map/ppermute | solution.py:35
  85.5 13.8 %collective-permute-start.14 = (bf16[3,1,1536]{2,0,1:T(4,128)(2,1)S(1)}, bf16[3,1,1536]{2,0,1:T(4,128)(2,1)S(1)}, u32[]{:S(2)}, u32[]{:S(2)}) collective-permute-start(bf16[3,1,1536]{2,0,1:T(4,128)(2,1)S(1)} %bitcast.252), channel_id=1, source_target_pairs={{0,13},{1,12},{2,15},{3,14},{4,9},{5,8},{6,11},{7,10},{8,5},{9,4},... | collective-permute-start | bytes 27656 | tf_op jit(solution)/shard_map/ppermute | solution.py:35
  87.5 11.9 %collective-permute-start.15 = (bf16[3,1,1536]{2,0,1:T(4,128)(2,1)S(1)}, bf16[3,1,1536]{2,0,1:T(4,128)(2,1)S(1)}, u32[]{:S(2)}, u32[]{:S(2)}) collective-permute-start(bf16[3,1,1536]{2,0,1:T(4,128)(2,1)S(1)} %bitcast.251), channel_id=1, source_target_pairs={{0,14},{1,15},{2,12},{3,13},{4,10},{5,11},{6,8},{7,9},{8,6},{9,7},... | collective-permute-start | bytes 27656 | tf_op jit(solution)/shard_map/ppermute | solution.py:35
  95.1 7.8 %collective-permute-start.16 = (bf16[3,1,1536]{2,0,1:T(4,128)(2,1)S(1)}, bf16[3,1,1536]{2,0,1:T(4,128)(2,1)S(1)}, u32[]{:S(2)}, u32[]{:S(2)}) collective-permute-start(bf16[3,1,1536]{2,0,1:T(4,128)(2,1)S(1)} %bitcast.250), channel_id=1, source_target_pairs={{0,15},{1,14},{2,13},{3,12},{4,11},{5,10},{6,9},{7,8},{8,7},{9,6},... | collective-permute-start | bytes 27656 | tf_op jit(solution)/shard_map/ppermute | solution.py:35
  105.7 5.4 %collective-permute-start.17 = (bf16[3,16,1024]{2,1,0:T(8,128)(2,1)S(1)}, bf16[3,16,1024]{2,1,0:T(8,128)(2,1)S(1)}, u32[]{:S(2)}, u32[]{:S(2)}) collective-permute-start(bf16[3,16,1024]{2,1,0:T(8,128)(2,1)S(1)} %get-tuple-element.41), channel_id=1, source_target_pairs={{0,1},{1,2},{2,3},{3,4},{4,5},{5,6},{6,7},{7,8},{8,9},{9,10},{10,1... | collective-permute-start | bytes 294920 | tf_op jit(solution)/shard_map/ppermute | solution.py:56
  107.6 7.5 %collective-permute-start.18 = (bf16[3,16,1024]{2,1,0:T(8,128)(2,1)S(1)}, bf16[3,16,1024]{2,1,0:T(8,128)(2,1)S(1)}, u32[]{:S(2)}, u32[]{:S(2)}) collective-permute-start(bf16[3,16,1024]{2,1,0:T(8,128)(2,1)S(1)} %get-tuple-element.40), channel_id=1, source_target_pairs={{1,0},{2,1},{3,2},{4,3},{5,4},{6,5},{7,6},{8,7},{9,8},{10,9},{11,1... | collective-permute-start | bytes 294920 | tf_op jit(solution)/shard_map/ppermute | solution.py:56
